TPU v7x, 256 devices: a whole 4x4x8 slice. The times are simulated.
256 devices in a mesh: sec: 2 (over y_lo), tp: 8 (over y_hi, x), dp: 16 (over z, core).
Axes of the slice: x: 4, y: 4 (y_hi: 2, y_lo: 2; y = y_hi * 2 + y_lo), z: 8, core: 2. Of those that a mesh axis runs over, the one named last changes fastest.
Arguments:
- student_input: bfloat16 [2048, 4096], P('dp', ('sec', 'tp')), may hold values from -6 to 6
- teacher_hidden: bfloat16 [2048, 16384], P('dp', ('sec', 'tp')), may hold values from -10 to 10
- projector: bfloat16 [16384, 4096], P(('sec', 'tp'), 'dp'), may hold values from -0.0625 to 0.0625
- gate_weight: bfloat16 [7168, 4096], P(('sec', 'tp')), may hold values from -0.09375 to 0.09375
- up_weight: bfloat16 [7168, 4096], P(('sec', 'tp')), may hold values from -0.09375 to 0.09375
- down_weight: bfloat16 [7168, 4096], P(('sec', 'tp')), may hold values from -0.0625 to 0.0625
Outputs:
- distill_loss: float32 [], replicated
- grad_gate: float32 [7168, 4096], P(('sec', 'tp'), 'dp')
- grad_up: float32 [7168, 4096], P(('sec', 'tp'), 'dp')
- grad_down: float32 [7168, 4096], P(('sec', 'tp'), 'dp')
All inputs are finite; a program needn't handle non-finite values.
Results may differ from a plain program's by a relative error of at most 0.0041.
Values may be sent and summed in bfloat16 or wider, within the bound.
No kernel may reach another device: no remote copies, remote signals or barrier semaphores. Data moves between devices by JAX's collectives and lax.ppermute only.
A program may use at most 128 MiB of HBM per device.

v0:
```python
import jax
import jax.numpy as jnp
from jax import lax
from jax.sharding import PartitionSpec as P

epsilon = 1e-05


def silu_parts(gate_val):
    sigma = jax.nn.sigmoid(gate_val)
    return (gate_val * sigma, sigma * (1.0 + gate_val * (1.0 - sigma)))


def contract_rows(left, right):
    return lax.dot_general(
        left, right, (((0,), (0,)), ((), ())), preferred_element_type=jnp.float32
    )


def contract_cols(left, right):
    return lax.dot_general(
        left, right, (((1,), (1,)), ((), ())), preferred_element_type=jnp.float32
    )


def shards(student_input, teacher_hidden, projector, gate_weight, up_weight, down_weight):
    row_count = student_input.shape[0]
    group_size = lax.axis_size(("sec", "tp"))
    tokens_all = row_count * lax.axis_size("dp")
    teacher_units = teacher_hidden.shape[1] * group_size
    inputs_full = lax.all_gather(student_input, ("sec", "tp"), axis=1, tiled=True)
    gate_val = contract_cols(inputs_full, gate_weight)
    up_val = contract_cols(inputs_full, up_weight)
    activated, slope_val = silu_parts(gate_val)
    hidden = (activated * up_val).astype(jnp.bfloat16)
    down_part = lax.psum_scatter(
        lax.dot_general(
            down_weight, hidden, (((0,), (1,)), ((), ())), preferred_element_type=jnp.float32
        ),
        ("sec", "tp"),
        scatter_dimension=0,
        tiled=True,
    )
    stream = student_input.astype(jnp.float32) + down_part.T
    projected = jnp.dot(
        teacher_hidden,
        lax.all_gather(projector, "dp", axis=1, tiled=True),
        preferred_element_type=jnp.float32,
    )
    teacher_float = teacher_hidden.astype(jnp.float32)
    squares = jnp.sum(teacher_float * teacher_float, axis=1)
    row_total = lax.psum(squares, ("sec", "tp"))
    target_part = lax.psum_scatter(projected, ("sec", "tp"), scatter_dimension=1, tiled=True)
    target = target_part / jnp.sqrt(row_total / teacher_units + epsilon)[:, None]
    mismatch = stream - target
    summed_loss = lax.psum(jnp.sum(mismatch * mismatch), ("sec", "tp", "dp"))
    loss_value = 0.5 * summed_loss / tokens_all
    outgrad_part = (mismatch / tokens_all).astype(jnp.bfloat16)
    outgrad_full = lax.all_gather(outgrad_part, ("sec", "tp"), axis=1, tiled=True)
    grad_hidden = contract_cols(outgrad_full, down_weight)
    grad_gate_in = (grad_hidden * up_val * slope_val).astype(jnp.bfloat16)
    grad_up_in = (grad_hidden * activated).astype(jnp.bfloat16)
    input_columns, outgrad_columns = (
        lax.all_to_all(inputs_full, "dp", split_axis=1, concat_axis=0, tiled=True),
        lax.all_to_all(outgrad_full, "dp", split_axis=1, concat_axis=0, tiled=True),
    )
    gate_rows, up_rows, hidden_rows = (
        lax.all_gather(grad_gate_in, "dp", axis=0, tiled=True),
        lax.all_gather(grad_up_in, "dp", axis=0, tiled=True),
        lax.all_gather(hidden, "dp", axis=0, tiled=True),
    )
    grad_gate = contract_rows(gate_rows, input_columns)
    grad_up = contract_rows(up_rows, input_columns)
    grad_down = contract_rows(hidden_rows, outgrad_columns)
    return (loss_value, grad_gate, grad_up, grad_down)


def solution(mesh):
    in_specs = (
        P("dp", ("sec", "tp")),
        P("dp", ("sec", "tp")),
        P(("sec", "tp"), "dp"),
        P(("sec", "tp"), None),
        P(("sec", "tp"), None),
        P(("sec", "tp"), None),
    )
    out_specs = (P(), P(("sec", "tp"), "dp"), P(("sec", "tp"), "dp"), P(("sec", "tp"), "dp"))
    return jax.shard_map(shards, mesh=mesh, in_specs=in_specs, out_specs=out_specs, check_vma=False)
```

profile of v0, /device:TPU:1, one launch (start us, length us, event | category | flops | bytes accessed | tf_op | source)
XLA Modules:
  0.0 558.0 jit_solution(12071474748263460014)
XLA Ops:
  7.2 0.0 all-gather.7.cloned.1.call-start
  7.2 1.6 copy.11
  8.8 0.0 all-gather.7.cloned.1.call-update
  8.8 0.0 all-gather.9.cloned.1.call-start
  8.9 0.7 all-gather.9.cloned.1.call-update
  9.6 0.0 reduce-scatter.3.cloned.1.call-start
  9.6 71.3 %all-gather.7.cloned.1.call-done = bf16[128,4096]{0,1:T(8,128)(2,1)} async-done(((bf16[128,256]{0,1:T(8,128)(2,1)}), bf16[128,4096]{0,1:T(8,128)(2,1)}) %all-gather.7.cloned.1.call-update) | async-done | bytes 1048592 | tf_op jit(solution)/shard_map/all_gather | solution.py:31
  81.0 3.6 fusion.7
  84.5 0.0 copy-done.4
  84.6 2.3 multiply_convert_fusion.2
  86.9 0.0 copy-start.2
  86.9 0.0 copy-start
  86.9 4.2 convolution_bitcast_fusion
  91.2 0.0 reduce-scatter.3.cloned.1.call-update
  91.2 0.0 copy-done.2
  91.2 0.0 copy-start.3
  91.2 0.0 reduce-scatter.5.cloned.1.call-start
  91.3 69.1 %all-gather.9.cloned.1.call-done = bf16[1024,4096]{1,0:T(8,128)(2,1)} async-done(((bf16[1024,256]{1,0:T(8,128)(2,1)}), bf16[1024,4096]{1,0:T(8,128)(2,1)}) %all-gather.9.cloned.1.call-update) | async-done | bytes 8388624 | tf_op jit(solution)/shard_map/all_gather | solution.py:47
  160.4 6.0 %fusion.3 = f32[128,4096]{1,0:T(8,128)} fusion(bf16[128,1024]{1,0:T(8,128)(2,1)S(1)} %copy-done, bf16[1024,4096]{1,0:T(8,128)(2,1)} %all-gather.9.cloned.1.call-done), kind=kOutput, calls=%fused_computation.13 | convolution fusion | flops 1073741824 | bytes 10747904 | tf_op jit(solution)/shard_map/dot_general | solution.py:45
  166.3 0.0 reduce-scatter.5.cloned.1.call-update
  166.4 0.0 all-gather.11.cloned.1.call-start
  166.4 0.1 multiply_reduce_fusion
  166.5 32.0 %psum.14 = f32[128]{0:T(128)S(1)} all-reduce(f32[128]{0:T(128)S(1)} %multiply_reduce_fusion), channel_id=1, replica_groups=mesh['sec'=2,'tp'=8,'dp'=16] {'sec','tp'}, use_global_device_ids=true, to_apply=%region_3.0 | all-reduce | flops 128 | bytes 1024 | tf_op jit(solution)/shard_map/psum | solution.py:52
  198.6 32.8 %reduce-scatter.3.cloned.1.call-done = f32[256,128]{0,1:T(8,128)} async-done(((f32[4096,128]{0,1:T(8,128)}), f32[256,128]{0,1:T(8,128)}) %reduce-scatter.3.cloned.1.call-update) | async-done | bytes 131088 | tf_op jit(solution)/shard_map/reduce_scatter | solution.py:36
  231.4 85.9 %reduce-scatter.5.cloned.1.call-done = f32[128,256]{1,0:T(8,128)} async-done(((f32[128,4096]{1,0:T(8,128)}), f32[128,256]{1,0:T(8,128)}) %reduce-scatter.5.cloned.1.call-update) | async-done | bytes 131088 | tf_op jit(solution)/shard_map/reduce_scatter | solution.py:53
  317.3 1.7 multiply_convert_fusion.3
  319.0 0.0 all-gather.11.cloned.1.call-update
  319.0 0.0 all-gather.17.cloned.1.call-start
  319.1 0.5 all-gather.17.cloned.1.call-update
  319.6 0.0 all-gather.15.cloned.1.call-start
  319.6 66.8 %all-gather.11.cloned.1.call-done = bf16[128,4096]{1,0:T(8,128)(2,1)} async-done(((bf16[128,256]{1,0:T(8,128)(2,1)}), bf16[128,4096]{1,0:T(8,128)(2,1)}) %all-gather.11.cloned.1.call-update) | async-done | bytes 1048592 | tf_op jit(solution)/shard_map/all_gather | solution.py:59
  386.5 4.2 multiply_convert_fusion
  390.7 0.0 all-gather.15.cloned.1.call-update
  390.7 18.8 %all-to-all-start = ((bf16[128,16,256]{0,2,1:T(8,128)(2,1)}), bf16[128,16,256]{0,2,1:T(8,128)(2,1)S(1)}, u32[]{:S(2)}, u32[]{:S(2)}) async-start(bf16[128,16,256]{0,2,1:T(8,128)(2,1)} %bitcast.2), calls=%async_computation.2 | async-start | bytes 2097152 | tf_op jit(solution)/shard_map/all_to_all | solution.py:64
  409.6 0.0 all-gather.13.cloned.1.call-start
  409.6 0.7 all-gather.13.cloned.1.call-update
  410.3 1.1 copy.16
  411.4 31.0 %all-to-all-done = bf16[128,16,256]{0,2,1:T(8,128)(2,1)S(1)} async-done(((bf16[128,16,256]{0,2,1:T(8,128)(2,1)}), bf16[128,16,256]{0,2,1:T(8,128)(2,1)S(1)}, u32[]{:S(2)}, u32[]{:S(2)}) %all-to-all-start) | async-done | bytes 1048608 | tf_op jit(solution)/shard_map/all_to_all | solution.py:64
  442.4 3.6 all-to-all-start.1
  446.0 0.6 multiply_reduce_fusion.1
  446.6 0.5 copy.12
  447.1 76.5 %psum.15 = f32[]{:T(128)} all-reduce(f32[]{:T(128)} %multiply_reduce_fusion.1), channel_id=1, replica_groups=mesh['sec'=2,'tp'=8,'dp'=16] {'sec','tp','dp'}, use_global_device_ids=true, to_apply=%region_5.0 | all-reduce | flops 1 | bytes 8 | tf_op jit(solution)/shard_map/psum | solution.py:56
  524.3 0.0 all-gather.17.cloned.1.call-done
  524.3 0.0 all-to-all-done.1
  524.3 2.9 fusion.6
  527.2 2.9 fusion.5
  530.2 17.0 %all-gather.13.cloned.1.call-done = bf16[2048,448]{0,1:T(8,128)(2,1)} async-done(((bf16[128,448]{0,1:T(8,128)(2,1)}), bf16[2048,448]{0,1:T(8,128)(2,1)}) %all-gather.13.cloned.1.call-update) | async-done | bytes 1835024 | tf_op jit(solution)/shard_map/all_gather | solution.py:68
  547.1 2.9 fusion.4
  (7 shorter events, 0.0 us)
Async XLA Ops:
  7.2 73.8 %all-gather.7.cloned.1.call-start = ((), (), s32[]{:S(2)}) async-start(), calls=%async_computation.4 | async-start | bytes 1114112 | tf_op jit(solution)/shard_map/all_gather | solution.py:31
  8.8 151.6 %all-gather.9.cloned.1.call-start = ((), (), s32[]{:S(2)}) async-start(), calls=%async_computation.6 | async-start | bytes 8912896 | tf_op jit(solution)/shard_map/all_gather | solution.py:47
  9.6 221.8 %reduce-scatter.3.cloned.1.call-start = ((), (), s32[]{:S(2)}) async-start(), calls=%async_computation.5 | async-start | bytes 2228224 | tf_op jit(solution)/shard_map/reduce_scatter | solution.py:36
  81.0 3.6 copy-start.4
  86.9 4.3 copy-start.2
  86.9 73.4 %copy-start = (bf16[128,1024]{1,0:T(8,128)(2,1)S(1)}, bf16[128,1024]{1,0:T(8,128)(2,1)}, u32[]{:S(2)}) copy-start(bf16[128,1024]{1,0:T(8,128)(2,1)} %param.7) | copy-start | bytes 786436
  91.2 226.1 %copy-start.3 = (bf16[128,256]{1,0:T(8,128)(2,1)S(1)}, bf16[128,256]{1,0:T(8,128)(2,1)}, u32[]{:S(2)}) copy-start(bf16[128,256]{1,0:T(8,128)(2,1)} %param.6) | copy-start | bytes 196612
  91.2 226.1 %reduce-scatter.5.cloned.1.call-start = ((), (), s32[]{:S(2)}) async-start(), calls=%async_computation.7 | async-start | bytes 2228224 | tf_op jit(solution)/shard_map/reduce_scatter | solution.py:53
  166.4 220.1 %all-gather.11.cloned.1.call-start = ((), (), s32[]{:S(2)}) async-start(), calls=%async_computation.8 | async-start | bytes 1114112 | tf_op jit(solution)/shard_map/all_gather | solution.py:59
  319.0 205.3 %all-gather.17.cloned.1.call-start = ((), (), s32[]{:S(2)}) async-start(), calls=%async_computation.11 | async-start | bytes 1949696 | tf_op jit(solution)/shard_map/all_gather | solution.py:70
  319.6 207.7 %all-gather.15.cloned.1.call-start = ((), (), s32[]{:S(2)}) async-start(), calls=%async_computation.10 | async-start | bytes 1949696 | tf_op jit(solution)/shard_map/all_gather | solution.py:69
  386.5 23.8 %copy-start.1 = (bf16[128,4096]{1,0:T(8,128)(2,1)S(1)}, bf16[128,4096]{1,0:T(8,128)(2,1)}, u32[]{:S(2)}) copy-start(bf16[128,4096]{1,0:T(8,128)(2,1)} %all-gather.11.cloned.1.call-done) | copy-start | bytes 3145732
  390.7 51.6 %all-to-all-start = ((bf16[128,16,256]{0,2,1:T(8,128)(2,1)}), bf16[128,16,256]{0,2,1:T(8,128)(2,1)S(1)}, u32[]{:S(2)}, u32[]{:S(2)}) async-start(bf16[128,16,256]{0,2,1:T(8,128)(2,1)} %bitcast.2), calls=%async_computation.2 | async-start | bytes 2097152 | tf_op jit(solution)/shard_map/all_to_all | solution.py:64
  409.6 137.6 %all-gather.13.cloned.1.call-start = ((), (), s32[]{:S(2)}) async-start(), calls=%async_computation.9 | async-start | bytes 1949696 | tf_op jit(solution)/shard_map/all_gather | solution.py:68
  442.4 81.9 %all-to-all-start.1 = ((bf16[128,16,256]{2,0,1:T(8,128)(2,1)}), bf16[128,16,256]{2,0,1:T(8,128)(2,1)S(1)}, u32[]{:S(2)}, u32[]{:S(2)}) async-start(bf16[128,16,256]{2,0,1:T(8,128)(2,1)} %bitcast.32), calls=%async_computation.3 | async-start | bytes 2097152 | tf_op jit(solution)/shard_map/all_to_all | solution.py:65
Sparse Core Ops, SparseCore 0:
  10.4 70.5 all-gather.6
  82.7 77.6 all-gather.8
  162.9 68.4 reduce-scatter.2
  233.8 83.4 reduce-scatter.4
  319.4 67.0 all-gather.10
  388.7 68.7 all-gather.16
  459.8 45.9 all-gather.14
  508.1 39.0 all-gather.12
where the time goes:
time: 559 us; the launch traced here: 558 us
  waiting for transfers between devices  376 us (67%)
  blocking collectives  109 us (19%)
  matrix products  29.1 us (5%)
  starting transfers between devices  22.7 us (4%)
  between operations  16 us (3%)
    reduce_scatter x1, waiting for transfers between devices, shards(): lax.psum_scatter(projected, ('sec', 'tp'), scatter_dimension=1, tiled=True)  85.9 us
    psum x1, blocking collectives, shards(): summed_loss = lax.psum(jnp.sum(mismatch * mismatch), ('sec', 'tp', 'dp'))  76.5 us
    all_gather x1, waiting for transfers between devices, shards(): lax.all_gather(student_input, ('sec', 'tp'), axis=1, tiled=True)  71.3 us
    all_gather x1, waiting for transfers between devices, shards(): lax.all_gather(projector, 'dp', axis=1, tiled=True)  69.1 us
    all_gather x1, waiting for transfers between devices, shards(): lax.all_gather(outgrad_part, ('sec', 'tp'), axis=1, tiled=True)  66.8 us
    reduce_scatter x1, waiting for transfers between devices, shards(): lax.psum_scatter(lax.dot_general(down_weight, hidden, (((0,), (1,)), ((),...  32.8 us
    psum x1, blocking collectives, shards(): row_total = lax.psum(squares, ('sec', 'tp'))  32 us
    all_to_all x1, waiting for transfers between devices, shards(): lax.all_to_all(inputs_full, 'dp', split_axis=1, concat_axis=0, tiled=True)  31 us
  transfers between devices with their start and end apart: 10, of which 7 were waited for; matrix products, arithmetic and copies ran while one was open for 5% of the time, Pallas kernels for 0%

commit v1 on v0

v1 whole, which is shorter than its diff:
```python
import jax
import jax.numpy as jnp
from jax import lax
from jax.sharding import PartitionSpec as P

epsilon = 1e-05

GROUP = ("sec", "tp")
EVERY = ("sec", "tp", "dp")
LINES = [[2 * z + c for z in range(8)] for c in range(2)]
SIBLING = [(d, d ^ 1) for d in range(16)]
SWAP = [
    (s * 16 + d, ((d & 14) | (s & 1)) * 16 + ((s & 14) | (d & 1)))
    for s in range(16)
    for d in range(16)
]


def silu_parts(gate_val):
    sigma = jax.nn.sigmoid(gate_val)
    return (gate_val * sigma, sigma * (1.0 + gate_val * (1.0 - sigma)))


def contract_rows(left, right):
    return lax.dot_general(
        left, right, (((0,), (0,)), ((), ())), preferred_element_type=jnp.float32
    )


def contract_cols(left, right):
    return lax.dot_general(
        left, right, (((1,), (1,)), ((), ())), preferred_element_type=jnp.float32
    )


def gather_group(block):
    copies = jnp.broadcast_to(block[None], (16,) + block.shape)
    return lax.all_to_all(copies, GROUP, 0, 0, tiled=True)


def gather_line(block):
    copies = jnp.broadcast_to(block[None], (8,) + block.shape)
    return lax.all_to_all(copies, "dp", 0, 0, axis_index_groups=LINES, tiled=True)


def scatter_sum(parts):
    return jnp.sum(
        lax.all_to_all(parts, GROUP, 0, 0, tiled=True).astype(jnp.float32), axis=0
    )


def split3(value):
    high = lax.reduce_precision(value, 8, 7)
    mid = lax.reduce_precision(value - high, 8, 7)
    low = value - high - mid
    return jnp.stack([high, mid, low]).astype(jnp.bfloat16)


def with_rows(block, extra):
    columns = block.shape[1]
    rows = jnp.pad(split3(extra), ((0, 13), (0, columns - extra.shape[0])))
    return jnp.concatenate([block, rows], axis=0)


def rows_of(blocks, tokens, count):
    rows = blocks[:, tokens : tokens + 3, :count].astype(jnp.float32)
    return jnp.sum(jnp.sum(rows, axis=1), axis=0)


def shards(student_input, teacher_hidden, projector, gate_weight, up_weight, down_weight):
    tokens, width = student_input.shape
    units = gate_weight.shape[0]
    tokens_all = tokens * 16
    teacher_units = teacher_hidden.shape[1] * 16
    core = lax.rem(lax.axis_index("dp"), 2)

    teacher_lines = lax.all_gather(
        teacher_hidden, "dp", axis=0, axis_index_groups=LINES, tiled=True
    )
    projector_other = lax.ppermute(projector, "dp", SIBLING)
    teacher_float = teacher_hidden.astype(jnp.float32)
    squares = jnp.sum(teacher_float * teacher_float, axis=1)

    gathered = gather_group(with_rows(student_input, squares))
    row_total = rows_of(gathered, tokens, tokens)
    inputs_full = gathered[:, :tokens].transpose(1, 0, 2).reshape(tokens, 16 * width)
    inputs_swapped = gather_group(lax.ppermute(student_input, EVERY, SWAP))

    gate_val = contract_cols(inputs_full, gate_weight)
    up_val = contract_cols(inputs_full, up_weight)
    activated, slope_val = silu_parts(gate_val)
    hidden = (activated * up_val).astype(jnp.bfloat16)
    gates = jnp.concatenate(
        [hidden, (up_val * slope_val).astype(jnp.bfloat16), activated.astype(jnp.bfloat16)],
        axis=1,
    )
    gates_lines = lax.all_gather(gates, "dp", axis=0, axis_index_groups=LINES, tiled=True)

    down_part = lax.dot_general(
        hidden,
        down_weight,
        (((1,), (0,)), ((), ())),
        preferred_element_type=jnp.float32,
    )
    down_part = down_part.reshape(tokens, 16, width).transpose(1, 0, 2).astype(jnp.bfloat16)
    stream = student_input.astype(jnp.float32) + scatter_sum(down_part)

    pair = jnp.where(
        core == 0,
        jnp.concatenate([projector, projector_other], axis=1),
        jnp.concatenate([projector_other, projector], axis=1),
    )
    projected = jnp.dot(teacher_lines, pair, preferred_element_type=jnp.float32)
    projected = projected.reshape(8, tokens, 2, width).transpose(0, 2, 1, 3)
    projected = projected.reshape(16, tokens, width).astype(jnp.bfloat16)
    target_part = lax.ppermute(scatter_sum(projected), EVERY, SWAP)
    target = target_part / jnp.sqrt(row_total / teacher_units + epsilon)[:, None]

    mismatch = stream - target
    summed_loss = jnp.sum(mismatch * mismatch)
    outgrad_part = (mismatch / tokens_all).astype(jnp.bfloat16)
    outgrad_gathered = gather_group(with_rows(outgrad_part, summed_loss[None]))
    group_loss = rows_of(outgrad_gathered, tokens, 1)
    outgrad_full = outgrad_gathered[:, :tokens].transpose(1, 0, 2).reshape(tokens, 16 * width)
    outgrad_swapped = gather_group(lax.ppermute(outgrad_part, EVERY, SWAP))

    grad_hidden = contract_cols(outgrad_full, down_weight).astype(jnp.bfloat16)
    hidden_gathered = gather_line(with_rows(grad_hidden, group_loss))
    line_loss = rows_of(hidden_gathered, tokens, 1)
    grad_hidden_lines = hidden_gathered[:, :tokens].reshape(8 * tokens, units).astype(jnp.float32)

    hidden_lines = gates_lines[:, :units]
    gate_lines = (grad_hidden_lines * gates_lines[:, units : 2 * units].astype(jnp.float32)).astype(
        jnp.bfloat16
    )
    up_lines = (grad_hidden_lines * gates_lines[:, 2 * units :].astype(jnp.float32)).astype(
        jnp.bfloat16
    )

    def columns_of(swapped):
        swapped = swapped.reshape(8, 2, tokens, width).transpose(0, 2, 1, 3)
        return swapped.reshape(8 * tokens, 2 * width)

    def finish(left, right):
        both = contract_rows(left, right)
        low, high = both[:, :width], both[:, width:]
        mine, theirs = jnp.where(core == 0, low, high), jnp.where(core == 0, high, low)
        return mine + lax.ppermute(theirs, "dp", SIBLING)

    grad_down = finish(hidden_lines, columns_of(outgrad_swapped))
    grad_gate = finish(gate_lines, columns_of(inputs_swapped))
    grad_up = finish(up_lines, columns_of(inputs_swapped))
    all_loss = line_loss + lax.ppermute(line_loss, "dp", SIBLING)
    loss_value = 0.5 * all_loss[0] / tokens_all
    return (loss_value, grad_gate, grad_up, grad_down)


def solution(mesh):
    in_specs = (
        P("dp", ("sec", "tp")),
        P("dp", ("sec", "tp")),
        P(("sec", "tp"), "dp"),
        P(("sec", "tp"), None),
        P(("sec", "tp"), None),
        P(("sec", "tp"), None),
    )
    out_specs = (P(), P(("sec", "tp"), "dp"), P(("sec", "tp"), "dp"), P(("sec", "tp"), "dp"))
    return jax.shard_map(shards, mesh=mesh, in_specs=in_specs, out_specs=out_specs, check_vma=False)
```

time: 559 us -> 232 us (0.42)
  waiting for transfers between devices: 376 us -> 74.1 us
  blocking collectives: 109 us -> 24.8 us
  starting transfers between devices: 22.7 us -> 61.5 us
  local copies, waits for them, and re-layouts: 3.23 us -> 14.8 us
  matrix products: 29.1 us -> 18.2 us
  between operations: 16 us -> 26.6 us
  other arithmetic: 2.47 us -> 10.6 us
    all_gather x6 -> x2, waiting for transfers between devices: 224 us -> 0.85 us  [the longest x1 0.83 us: shards(): lax.all_gather(teacher_hidden, 'dp', axis=0, axis_index_groups=LINES, til...]
    reduce_scatter x2 -> x0, waiting for transfers between devices: 119 us -> none  [the longest x1 85.9 us: shards(): lax.psum_scatter(projected, ('sec', 'tp'), scatter_dimension=1, tiled=True)]
    psum x2 -> x0, blocking collectives: 109 us -> none  [the longest x1 76.5 us: shards(): summed_loss = lax.psum(jnp.sum(mismatch * mismatch), ('sec', 'tp', 'dp'))]
    all_to_all x2 -> x6, waiting for transfers between devices: 31 us -> 70 us  [the longest x3 27.3 us: gather_group(): return lax.all_to_all(copies, GROUP, 0, 0, tiled=True)]
    all_to_all x2 -> x6, starting transfers between devices: 22.4 us -> 53.9 us  [the longest x3 34.7 us: gather_group(): return lax.all_to_all(copies, GROUP, 0, 0, tiled=True)]
    all_to_all x0 -> x1, blocking collectives: none -> 24.8 us  [gather_group(): return lax.all_to_all(copies, GROUP, 0, 0, tiled=True)]
    ppermute x0 -> x8, starting transfers between devices: none -> 7.52 us  [the longest x3 2.93 us: finish(): return mine + lax.ppermute(theirs, 'dp', SIBLING)]
    dot_general x2, matrix products: 10.2 us -> 3.64 us  [the longest x1 2.89 us: shards(): projected = jnp.dot(teacher_lines, pair, preferred_element_type=jnp.float32)]
  transfers between devices with their start and end apart: 10 -> 16, of which waited for: 7 -> 9; matrix products, arithmetic and copies ran while one was open for 5% -> 18% of each run, Pallas kernels for 0% -> 0%
where the time goes in v1:
time: 232 us; the launch traced here: 231 us
  waiting for transfers between devices  74.1 us (32%)
  starting transfers between devices  61.5 us (27%)
  between operations  26.6 us (11%)
  blocking collectives  24.8 us (11%)
  matrix products  18.2 us (8%)
  local copies, waits for them, and re-layouts  14.8 us (6%)
  other arithmetic  10.6 us (5%)
    all_to_all x3, starting transfers between devices, gather_group(): return lax.all_to_all(copies, GROUP, 0, 0, tiled=True)  34.7 us
    all_to_all x3, waiting for transfers between devices, gather_group(): return lax.all_to_all(copies, GROUP, 0, 0, tiled=True)  27.3 us
    all_to_all x1, waiting for transfers between devices, gather_line(): lax.all_to_all(copies, 'dp', 0, 0, axis_index_groups=LINES, tiled=True)  24.8 us
    all_to_all x1, blocking collectives, gather_group(): return lax.all_to_all(copies, GROUP, 0, 0, tiled=True)  24.8 us
    all_to_all x2, waiting for transfers between devices, scatter_sum(): lax.all_to_all(parts, GROUP, 0, 0, tiled=True).astype(jnp.float32)  17.9 us
    all_to_all x1, starting transfers between devices, gather_line(): lax.all_to_all(copies, 'dp', 0, 0, axis_index_groups=LINES, tiled=True)  11.8 us
    dot_general x3, matrix products, contract_cols(): lax.dot_general(left, right, (((1,), (1,)), ((), ())), preferred_element_...  8.25 us
    all_to_all x2, starting transfers between devices, scatter_sum(): lax.all_to_all(parts, GROUP, 0, 0, tiled=True).astype(jnp.float32)  7.46 us
  transfers between devices with their start and end apart: 16, of which 9 were waited for; matrix products, arithmetic and copies ran while one was open for 18% of the time, Pallas kernels for 0%

profile of v1, /device:TPU:1, one launch (start us, length us, event | category | flops | bytes accessed | tf_op | source)
XLA Modules:
  0.0 230.6 jit_solution(5423727571558195566)
XLA Ops:
  7.2 0.7 all-gather.3.cloned.1.call-update
  7.9 1.1 multiply_reduce_fusion
  9.0 0.8 pad_maximum_fusion.2
  9.9 24.8 %all_to_all.35 = bf16[16,144,256]{2,1,0:T(8,128)(2,1)S(1)} all-to-all(bf16[16,144,256]{2,1,0:T(8,128)(2,1)S(1)} %broadcast_in_dim.12), channel_id=1, replica_groups=mesh['sec'=2,'tp'=8,'dp'=16] {'sec','tp'}, dimensions={0} | all-to-all | bytes 2359296 | tf_op jit(solution)/shard_map/all_to_all | solution.py:38
  35.5 3.3 %fusion.54 = f32[128,448]{0,1:T(8,128)S(1)} fusion(bf16[448,4096]{1,0:T(8,128)(2,1)} %param.9, bf16[128,4096]{0,1:T(8,128)(2,1)S(1)} %bitcast.91), kind=kOutput, calls=%fused_computation.92 | convolution fusion | flops 469762048 | bytes 4947968 | tf_op jit(solution)/shard_map/dot_general | solution.py:31
  38.9 1.8 multiply_convert_fusion
  41.0 0.7 convolution_convert_fusion
  41.8 1.1 copy.68
  42.9 3.7 %all-to-all-start.1 = ((bf16[16,128,256]{2,1,0:T(8,128)(2,1)}), bf16[16,128,256]{2,1,0:T(8,128)(2,1)S(1)}, u32[]{:S(2)}, u32[]{:S(2)}) async-start(bf16[16,128,256]{2,1,0:T(8,128)(2,1)} %bitcast.85), calls=%async_computation.1 | async-start | bytes 2097152 | tf_op jit(solution)/shard_map/all_to_all | solution.py:48
  46.5 2.1 collective-permute-start
  48.7 1.5 collective-permute-done
  50.2 0.8 all-gather.3.cloned.1.call-done
  51.0 2.9 %fusion.2 = bf16[64,8,8,128]{3,1,2,0:T(8,128)(2,1)S(1)} fusion(bf16[1024,1024]{1,0:T(8,128)(2,1)} %all-gather.3.cloned.1.call-done, bf16[1024,256]{1,0:T(8,128)(2,1)S(1)} %collective-permute-done, bf16[1024,256]{1,0:T(8,128)(2,1)S(1)} %copy-done.5, pred[]{:T(512)S(6)} %eq.2), kind=kOutput, calls=%fused_computation.9 | convolution fusion | flops 1078984704 | bytes 4194305 | tf_op jit(solution)/shard_map/dot_general | solution.py:113
  54.2 1.5 copy.36
  55.7 6.2 %all-to-all-done.1 = bf16[16,128,256]{2,1,0:T(8,128)(2,1)S(1)} async-done(((bf16[16,128,256]{2,1,0:T(8,128)(2,1)}), bf16[16,128,256]{2,1,0:T(8,128)(2,1)S(1)}, u32[]{:S(2)}, u32[]{:S(2)}) %all-to-all-start.1) | async-done | bytes 1048608 | tf_op jit(solution)/shard_map/all_to_all | solution.py:48
  61.9 3.8 %all-to-all-start.2 = ((bf16[16,128,256]{2,1,0:T(8,128)(2,1)}), bf16[16,128,256]{2,1,0:T(8,128)(2,1)S(1)}, u32[]{:S(2)}, u32[]{:S(2)}) async-start(bf16[16,128,256]{2,1,0:T(8,128)(2,1)} %bitcast.89), calls=%async_computation.2 | async-start | bytes 2097152 | tf_op jit(solution)/shard_map/all_to_all | solution.py:48
  65.8 1.7 pad_maximum_fusion
  67.5 0.7 collective-permute-start.3
  68.2 11.7 %all-to-all-done.2 = bf16[16,128,256]{2,1,0:T(8,128)(2,1)S(1)} async-done(((bf16[16,128,256]{2,1,0:T(8,128)(2,1)}), bf16[16,128,256]{2,1,0:T(8,128)(2,1)S(1)}, u32[]{:S(2)}, u32[]{:S(2)}) %all-to-all-start.2) | async-done | bytes 1048608 | tf_op jit(solution)/shard_map/all_to_all | solution.py:48
  79.9 1.1 broadcast_in_dim.16
  81.0 7.3 %all-to-all-start.5 = ((bf16[16,128,256]{2,1,0:T(8,128)(2,1)}), bf16[16,128,256]{2,1,0:T(8,128)(2,1)S(1)}, u32[]{:S(2)}, u32[]{:S(2)}) async-start(bf16[16,128,256]{2,1,0:T(8,128)(2,1)} %broadcast_in_dim.16), calls=%async_computation.5 | async-start | bytes 2097152 | tf_op jit(solution)/shard_map/all_to_all | solution.py:38
  88.5 0.7 collective-permute-start.1
  95.0 7.9 %all-to-all-done.5 = bf16[16,128,256]{2,1,0:T(8,128)(2,1)S(1)} async-done(((bf16[16,128,256]{2,1,0:T(8,128)(2,1)}), bf16[16,128,256]{2,1,0:T(8,128)(2,1)S(1)}, u32[]{:S(2)}, u32[]{:S(2)}) %all-to-all-start.5) | async-done | bytes 1048608 | tf_op jit(solution)/shard_map/all_to_all | solution.py:38
  102.9 1.1 broadcast_in_dim.14
  104.0 20.5 %all-to-all-start.3 = ((bf16[16,144,256]{2,1,0:T(8,128)(2,1)}), bf16[16,144,256]{2,1,0:T(8,128)(2,1)S(1)}, u32[]{:S(2)}, u32[]{:S(2)}) async-start(bf16[16,144,256]{2,1,0:T(8,128)(2,1)} %broadcast_in_dim.14), calls=%async_computation.3 | async-start | bytes 2359296 | tf_op jit(solution)/shard_map/all_to_all | solution.py:38
  124.5 0.7 collective-permute-start.6
  125.2 16.1 %all-to-all-done.3 = bf16[16,144,256]{2,1,0:T(8,128)(2,1)S(1)} async-done(((bf16[16,144,256]{2,1,0:T(8,128)(2,1)}), bf16[16,144,256]{2,1,0:T(8,128)(2,1)S(1)}, u32[]{:S(2)}, u32[]{:S(2)}) %all-to-all-start.3) | async-done | bytes 1179680 | tf_op jit(solution)/shard_map/all_to_all | solution.py:38
  141.3 1.1 broadcast_in_dim.17
  142.4 6.8 %all-to-all-start.6 = ((bf16[16,128,256]{2,1,0:T(8,128)(2,1)}), bf16[16,128,256]{2,1,0:T(8,128)(2,1)S(1)}, u32[]{:S(2)}, u32[]{:S(2)}) async-start(bf16[16,128,256]{2,1,0:T(8,128)(2,1)} %broadcast_in_dim.17), calls=%async_computation.6 | async-start | bytes 2097152 | tf_op jit(solution)/shard_map/all_to_all | solution.py:38
  154.8 1.1 slice.62
  155.8 1.6 copy.44
  157.5 3.1 %convolution_convert_fusion.2 = bf16[128,448]{0,1:T(8,128)(2,1)S(1)} fusion(bf16[448,4096]{1,0:T(8,128)(2,1)} %param.11, bf16[128,4096]{0,1:T(8,128)(2,1)S(1)} %bitcast.95), kind=kOutput, calls=%fused_computation.10 | convolution fusion | flops 469819392 | bytes 4833280 | tf_op jit(solution)/shard_map/dot_general | solution.py:31
  160.9 3.3 %all-to-all-done.6 = bf16[16,128,256]{2,1,0:T(8,128)(2,1)S(1)} async-done(((bf16[16,128,256]{2,1,0:T(8,128)(2,1)}), bf16[16,128,256]{2,1,0:T(8,128)(2,1)S(1)}, u32[]{:S(2)}, u32[]{:S(2)}) %all-to-all-start.6) | async-done | bytes 1048608 | tf_op jit(solution)/shard_map/all_to_all | solution.py:38
  164.1 1.1 broadcast_in_dim.15
  165.2 11.8 %all-to-all-start.4 = ((bf16[8,144,448]{2,1,0:T(8,128)(2,1)}), bf16[8,144,448]{2,1,0:T(8,128)(2,1)S(1)}, u32[]{:S(2)}, u32[]{:S(2)}) async-start(bf16[8,144,448]{2,1,0:T(8,128)(2,1)} %broadcast_in_dim.15), calls=%async_computation.4 | async-start | bytes 2359296 | tf_op jit(solution)/shard_map/all_to_all | solution.py:43
  177.0 1.5 copy.41
  178.5 0.7 copy.42
  179.3 1.9 fusion.3
  181.1 0.8 slice_select_fusion
  182.0 2.2 collective-permute-start.7
  184.2 24.8 %all-to-all-done.4 = bf16[8,144,448]{2,1,0:T(8,128)(2,1)S(1)} async-done(((bf16[8,144,448]{2,1,0:T(8,128)(2,1)}), bf16[8,144,448]{2,1,0:T(8,128)(2,1)S(1)}, u32[]{:S(2)}, u32[]{:S(2)}) %all-to-all-start.4) | async-done | bytes 1032224 | tf_op jit(solution)/shard_map/all_to_all | solution.py:43
  209.1 1.3 copy.45
  210.4 2.6 %fusion.8 = f32[448,512]{1,0:T(8,128)S(1)} fusion(bf16[64,8,8,128]{3,2,1,0:T(8,128)(2,1)} %bitcast.93, bf16[1024,1344]{0,1:T(8,128)(2,1)} %all-gather.5.cloned.1.call-done, bf16[8,128,448]{1,2,0:T(8,128)(2,1)} %copy.45), kind=kOutput, calls=%fused_computation.16 | convolution fusion | flops 471597056 | bytes 3801088 | tf_op jit(solution)/shard_map/dot_general | solution.py:25
  213.7 1.9 fusion.6
  215.7 1.9 select_add_fusion
  218.7 1.0 collective-permute-done.2
  220.9 0.9 select_add_fusion.2
  221.8 0.9 select_add_fusion.1
  (47 shorter events, 5.6 us)
Async XLA Ops:
  7.2 43.9 %all-gather.3.cloned.1.call-start = ((), (), s32[]{:S(2)}) async-start(), calls=%async_computation.7 | async-start | bytes 2359296 | tf_op jit(solution)/shard_map/all_gather | solution.py:77
  35.5 3.3 %copy-start.4 = (bf16[448,4096]{1,0:T(8,128)(2,1)S(1)}, bf16[448,4096]{1,0:T(8,128)(2,1)}, u32[]{:S(2)}) copy-start(bf16[448,4096]{1,0:T(8,128)(2,1)} %param.10) | copy-start | bytes 11010052
  38.9 2.2 copy-start
  41.8 4.8 %copy-start.5 = (bf16[1024,256]{1,0:T(8,128)(2,1)S(1)}, bf16[1024,256]{1,0:T(8,128)(2,1)}, u32[]{:S(2)}) copy-start(bf16[1024,256]{1,0:T(8,128)(2,1)} %param.8) | copy-start | bytes 1572868
  42.9 19.1 %all-to-all-start.1 = ((bf16[16,128,256]{2,1,0:T(8,128)(2,1)}), bf16[16,128,256]{2,1,0:T(8,128)(2,1)S(1)}, u32[]{:S(2)}, u32[]{:S(2)}) async-start(bf16[16,128,256]{2,1,0:T(8,128)(2,1)} %bitcast.85), calls=%async_computation.1 | async-start | bytes 2097152 | tf_op jit(solution)/shard_map/all_to_all | solution.py:48
  46.5 3.7 %collective-permute-start = (bf16[1024,256]{1,0:T(8,128)(2,1)S(1)}, bf16[1024,256]{1,0:T(8,128)(2,1)S(1)}, u32[]{:S(2)}, u32[]{:S(2)}) collective-permute-start(bf16[1024,256]{1,0:T(8,128)(2,1)S(1)} %copy-done.5), channel_id=1, source_target_pairs={{0,1},{1,0},{2,3},{3,2},{4,5},{5,4},{6,7},{7,6},{8,9},{9,8},{10,11... | collective-permute-start | bytes 1572872 | tf_op jit(solution)/shard_map/ppermute | solution.py:80
  54.2 13.3 %copy-start.3 = (bf16[128,256]{1,0:T(8,128)(2,1)S(1)}, bf16[128,256]{1,0:T(8,128)(2,1)}, u32[]{:S(2)}) copy-start(bf16[128,256]{1,0:T(8,128)(2,1)} %param.6) | copy-start | bytes 196612
  61.9 18.0 %all-to-all-start.2 = ((bf16[16,128,256]{2,1,0:T(8,128)(2,1)}), bf16[16,128,256]{2,1,0:T(8,128)(2,1)S(1)}, u32[]{:S(2)}, u32[]{:S(2)}) async-start(bf16[16,128,256]{2,1,0:T(8,128)(2,1)} %bitcast.89), calls=%async_computation.2 | async-start | bytes 2097152 | tf_op jit(solution)/shard_map/all_to_all | solution.py:48
  65.7 113.5 %all-gather.5.cloned.1.call-start = ((), (), s32[]{:S(2)}) async-start(), calls=%async_computation.8 | async-start | bytes 3096576 | tf_op jit(solution)/shard_map/all_gather | solution.py:97
  67.5 0.7 collective-permute-start.3
  81.0 21.9 %all-to-all-start.5 = ((bf16[16,128,256]{2,1,0:T(8,128)(2,1)}), bf16[16,128,256]{2,1,0:T(8,128)(2,1)S(1)}, u32[]{:S(2)}, u32[]{:S(2)}) async-start(bf16[16,128,256]{2,1,0:T(8,128)(2,1)} %broadcast_in_dim.16), calls=%async_computation.5 | async-start | bytes 2097152 | tf_op jit(solution)/shard_map/all_to_all | solution.py:38
  88.5 0.8 collective-permute-start.1
  104.0 37.3 %all-to-all-start.3 = ((bf16[16,144,256]{2,1,0:T(8,128)(2,1)}), bf16[16,144,256]{2,1,0:T(8,128)(2,1)S(1)}, u32[]{:S(2)}, u32[]{:S(2)}) async-start(bf16[16,144,256]{2,1,0:T(8,128)(2,1)} %broadcast_in_dim.14), calls=%async_computation.3 | async-start | bytes 2359296 | tf_op jit(solution)/shard_map/all_to_all | solution.py:38
  124.5 0.7 collective-permute-start.6
  142.4 21.7 %all-to-all-start.6 = ((bf16[16,128,256]{2,1,0:T(8,128)(2,1)}), bf16[16,128,256]{2,1,0:T(8,128)(2,1)S(1)}, u32[]{:S(2)}, u32[]{:S(2)}) async-start(bf16[16,128,256]{2,1,0:T(8,128)(2,1)} %broadcast_in_dim.17), calls=%async_computation.6 | async-start | bytes 2097152 | tf_op jit(solution)/shard_map/all_to_all | solution.py:38
  165.2 43.8 %all-to-all-start.4 = ((bf16[8,144,448]{2,1,0:T(8,128)(2,1)}), bf16[8,144,448]{2,1,0:T(8,128)(2,1)S(1)}, u32[]{:S(2)}, u32[]{:S(2)}) async-start(bf16[8,144,448]{2,1,0:T(8,128)(2,1)} %broadcast_in_dim.15), calls=%async_computation.4 | async-start | bytes 2359296 | tf_op jit(solution)/shard_map/all_to_all | solution.py:43
  182.0 33.8 %collective-permute-start.7 = (f32[448,256]{1,0:T(8,128)}, f32[448,256]{1,0:T(8,128)}, u32[]{:S(2)}, u32[]{:S(2)}) collective-permute-start(f32[448,256]{1,0:T(8,128)} %slice_select_fusion), channel_id=1, source_target_pairs={{0,1},{1,0},{2,3},{3,2},{4,5},{5,4},{6,7},{7,6},{8,9},{9,8},{10,11... | collective-permute-start | bytes 1376264 | tf_op jit(solution)/shard_map/ppermute | solution.py:148
  210.4 3.3 %copy-start.1 = (bf16[8,128,2,256]{1,0,3,2:T(8,128)(2,1)S(1)}, bf16[8,128,2,256]{1,0,3,2:T(8,128)(2,1)}, u32[]{:S(2)}) copy-start(bf16[8,128,2,256]{1,0,3,2:T(8,128)(2,1)} %copy.41) | copy-start | bytes 3145732
  210.4 3.3 %copy-start.2 = (bf16[8,128,448]{1,2,0:T(8,128)(2,1)S(1)}, bf16[8,128,448]{1,2,0:T(8,128)(2,1)}, u32[]{:S(2)}) copy-start(bf16[8,128,448]{1,2,0:T(8,128)(2,1)} %copy.45) | copy-start | bytes 2752516
  213.1 7.9 %collective-permute-start.4 = (f32[448,256]{1,0:T(8,128)S(1)}, f32[448,256]{1,0:T(8,128)S(1)}, u32[]{:S(2)}, u32[]{:S(2)}) collective-permute-start(f32[448,256]{1,0:T(8,128)S(1)} %slice_select_fusion.2), channel_id=1, source_target_pairs={{0,1},{1,0},{2,3},{3,2},{4,5},{5,4},{6,7},{7,6},{8,9},{9,8},{10,11... | collective-permute-start | bytes 1376264 | tf_op jit(solution)/shard_map/ppermute | solution.py:148
  215.6 6.2 %collective-permute-start.5 = (f32[448,256]{1,0:T(8,128)S(1)}, f32[448,256]{1,0:T(8,128)S(1)}, u32[]{:S(2)}, u32[]{:S(2)}) collective-permute-start(f32[448,256]{1,0:T(8,128)S(1)} %slice_select_fusion.1), channel_id=1, source_target_pairs={{0,1},{1,0},{2,3},{3,2},{4,5},{5,4},{6,7},{7,6},{8,9},{9,8},{10,11... | collective-permute-start | bytes 1376264 | tf_op jit(solution)/shard_map/ppermute | solution.py:148
  218.2 1.4 collective-permute-start.2
Sparse Core Ops, SparseCore 0:
  9.8 41.1 all-gather.2
  68.9 61.7 all-gather.4
